TPU v7x, 32 devices: a whole 2x2x4 slice. The times are simulated.
32 devices in a mesh: sec: 2 (over x), ty: 4 (over y, core), tx: 4 (over z).
Axes of the slice: x: 2, y: 2, z: 4, core: 2. Of those that a mesh axis runs over, the one named last changes fastest.
Arguments:
- descriptors: bfloat16 [2, 4, 4, 1024, 128], P('sec', 'ty', 'tx'), may hold values from -4 to 4, as said below
- positions: bfloat16 [2, 4, 4, 2, 1024], P('sec', 'ty', 'tx'), may hold values from -1 to 1
- vertex_ids: int32 [2, 4, 4, 1024], P('sec', 'ty', 'tx'), may hold values from 0 to 262143, as said below
- candidate_blocks: int32 [2, 4, 4, 32], P('sec', 'ty', 'tx'), may hold values from 0 to 127, as said below
- candidate_count: int32 [2, 4, 4], P('sec', 'ty', 'tx'), may hold values from 8 to 32, as said below
- displacement: float32 [2, 2, 512, 512], P('sec', None, 'ty', 'tx'), may hold values from -3 to 3
- stiffness: float32 [2, 512, 512], P('sec', 'ty', 'tx'), may hold values from 0.25 to 4
Outputs:
- relaxed: float32 [2, 2, 512, 512], P('sec', None, 'ty', 'tx')
Inputs may be any that keep to these rules, and one draw needn't show every extreme that they name: `descriptors`: descriptor entries stay within the range. `candidate_blocks`: A list names distinct blocks tile * 8 + j of the next section; among its live entries at most 4 blocks come from any one tile, and some list has 4 live blocks of one tile. `candidate_count`: some tile has all 32 entries live. `vertex_ids`: ids follow the vertex numbering of the steps, anywhere in the section.
All inputs are finite; a program needn't handle non-finite values.
Results may differ from a plain program's by a relative error of at most 0.0019.
Values may be sent and summed in bfloat16 or wider, within the bound.
No kernel may reach another device: no remote copies, remote signals or barrier semaphores. Data moves between devices by JAX's collectives and lax.ppermute only.
A program may use at most 192 MiB of HBM per device.

v0:
```python
import functools
import math

import jax
import jax.numpy as jnp
from jax import lax
from jax.experimental import pallas as pl
from jax.experimental.pallas import tpu as pltpu
from jax.sharding import PartitionSpec as P

BLK = 128
ITERS = 4
LANES = 128
PLACE_ROWS = 16
VMEM_BYTES = 24 * 1024 * 1024

spring_sec = 0.5
spring_match = 1.0
relax_rate = 0.8


def passed_along(value, axis, by):
    devices = lax.axis_size(axis)
    pairs = [(i, i + by) for i in range(devices) if 0 <= i + by < devices]
    return lax.ppermute(value, axis, pairs)


def exchanged(value, axes):
    return lax.all_to_all(value, axes, split_axis=0, concat_axis=0, tiled=True)


def spread(value, axes):
    copies = jnp.broadcast_to(value[None], (lax.axis_size(axes),) + value.shape)
    return exchanged(copies, axes)


def nt_dot(a, b):
    return lax.dot_general(a, b, (((1,), (1,)), ((), ())), preferred_element_type=jnp.float32)


def in_vmem(count):
    return [pl.BlockSpec(memory_space=pltpu.VMEM)] * count


def in_smem():
    return pl.BlockSpec(memory_space=pltpu.SMEM)


def match_kernel(scale, work_ref, query_ref, key_ref, out_ref, place_buf):
    shares, tile_rows, out_rows, _ = out_ref.shape
    rows = out_rows // 4
    point_total = shares * rows * LANES
    key_tiles = key_ref.shape[0]
    key_rows = key_ref.shape[1] - PLACE_ROWS
    part = key_rows // BLK
    total = key_tiles * part
    step = 256 if point_total % 256 == 0 else LANES

    row_at = lax.broadcasted_iota(jnp.int32, (PLACE_ROWS, LANES), 0)
    for tile in range(key_tiles):
        place = key_ref[tile, pl.ds(key_rows, PLACE_ROWS), :].astype(jnp.float32)
        for j in range(part):
            x, y = place[j : j + 1, :], place[part + j : part + j + 1, :]
            stacked = jnp.where(
                row_at == 0, x, jnp.where(row_at == 1, y, jnp.where(row_at == 2, 1.0, 0.0))
            )
            place_buf[tile * part + j] = stacked.astype(jnp.bfloat16)

    for tile in range(tile_rows):
        count = work_ref[tile, total]

        def body(pair, carry):
            tops, sums = carry
            live = 2 * pair + 1 < count
            first = work_ref[tile, 2 * pair]
            second = work_ref[tile, jnp.where(live, 2 * pair + 1, 2 * pair)]

            def keys_of(block):
                at = pl.multiple_of(lax.rem(block, part) * BLK, BLK)
                return key_ref[lax.div(block, part), pl.ds(at, BLK), :]

            keys = jnp.concatenate([keys_of(first), keys_of(second)], axis=0)
            kept = jnp.where(live, 1.0, 0.0).astype(jnp.bfloat16)
            place = jnp.concatenate([place_buf[first], place_buf[second] * kept], axis=1)
            new_tops, new_sums = [], []
            for c in range(point_total // step):
                queries = query_ref[tile, pl.ds(c * step, step), :]
                scores = nt_dot(keys, queries) * scale
                top = jnp.maximum(tops[c], jnp.max(scores, axis=0, keepdims=True))
                weights = jnp.exp2(scores - top).astype(jnp.bfloat16)
                added = jnp.dot(place, weights, preferred_element_type=jnp.float32)
                new_tops.append(top)
                new_sums.append(sums[c] * jnp.exp2(tops[c] - top) + added)
            return tuple(new_tops), tuple(new_sums)

        chunks = point_total // step
        tops, sums = lax.fori_loop(
            0,
            (count + 1) // 2,
            body,
            (
                tuple(jnp.full((1, step), -1e30, jnp.float32) for _ in range(chunks)),
                tuple(jnp.zeros((PLACE_ROWS, step), jnp.float32) for _ in range(chunks)),
            ),
        )
        per_chunk = step // LANES
        for row in range(shares * rows):
            c, lanes = row // per_chunk, slice((row % per_chunk) * LANES, (row % per_chunk + 1) * LANES)
            share, at = row // rows, row % rows
            for place, value in enumerate(
                (tops[c][:, lanes], sums[c][2:3, lanes], sums[c][0:1, lanes], sums[c][1:2, lanes])
            ):
                out_ref[share, tile, pl.ds(place * rows + at, 1), :] = value


def match(work, queries, keys, score_factor, shares, point_total):
    tile_rows = queries.shape[0]
    width = queries.shape[2]
    key_tiles = keys.shape[0]
    part = (keys.shape[1] - PLACE_ROWS) // BLK
    rows = point_total // LANES // shares
    pairs = tile_rows * key_tiles * part
    return pl.pallas_call(
        functools.partial(match_kernel, score_factor * math.log2(math.e)),
        out_shape=jax.ShapeDtypeStruct((shares, tile_rows, 4 * rows, LANES), jnp.float32),
        in_specs=[in_smem()] + in_vmem(2),
        out_specs=pl.BlockSpec(memory_space=pltpu.VMEM),
        scratch_shapes=[pltpu.VMEM((key_tiles * part, PLACE_ROWS, LANES), jnp.bfloat16)],
        compiler_params=pltpu.CompilerParams(vmem_limit_bytes=VMEM_BYTES),
        cost_estimate=pl.CostEstimate(
            flops=pairs * point_total * BLK * width,
            bytes_accessed=2 * (queries.size + keys.size),
            transcendentals=pairs * point_total * BLK // 4,
        ),
        name="match",
    )(work, queries, keys)


def combine_kernel(parts_ref, place_ref, out_ref):
    parts, out_rows, _ = parts_ref.shape
    rows = out_rows // 4
    tops = [parts_ref[i, 0:rows, :] for i in range(parts)]
    top = functools.reduce(jnp.maximum, tops)
    total = x = y = jnp.zeros_like(top)
    for i in range(parts):
        gain = jnp.exp2(tops[i] - top)
        total += gain * parts_ref[i, rows : 2 * rows, :]
        x += gain * parts_ref[i, 2 * rows : 3 * rows, :]
        y += gain * parts_ref[i, 3 * rows :, :]
    pull = jnp.concatenate([x / total, y / total], axis=0) - place_ref[...].astype(jnp.float32)
    for i in range(out_ref.shape[0]):
        out_ref[i] = pull


def combine(parts, place, copies):
    return pl.pallas_call(
        combine_kernel,
        out_shape=jax.ShapeDtypeStruct((copies,) + place.shape, jnp.float32),
        in_specs=in_vmem(2),
        out_specs=pl.BlockSpec(memory_space=pltpu.VMEM),
        name="combine",
    )(parts, place)


def vertex_sums(side, halo, tile_cols, at_ref, ids_ref, points_ref, sum_ref):
    span = side + 2 * halo
    tall = -(-span // 16) * 16
    wide = sum_ref.shape[2]
    shares, tiles, both_rows, _ = points_ref.shape
    rows = both_rows // 2
    along = functools.partial(jnp.concatenate, axis=1)

    def folded(at):
        return jnp.where(
            (at >= 0) & (at < side + halo), at, jnp.where((at < 0) & (at >= -halo), at + span, -1)
        )

    sum_ref[...] = jnp.zeros_like(sum_ref)

    @pl.loop(0, tiles)
    def _(tile):
        ids = ids_ref[tile]
        tile_of = lax.div(ids, side * side)
        within = lax.rem(ids, side * side)
        row = folded(lax.div(tile_of, tile_cols) * side + lax.div(within, side) - at_ref[0])
        col = folded(lax.rem(tile_of, tile_cols) * side + lax.rem(within, side) - at_ref[1])
        values = [points_ref[share, tile] for share in range(shares)]
        x = along([v[i : i + 1, :] for v in values for i in range(rows)])
        y = along([v[i : i + 1, :] for v in values for i in range(rows, 2 * rows)])
        row, col = (along([v[i : i + 1, :] for i in range(shares * rows)]) for v in (row, col))
        count = row.shape[1]
        at = lax.broadcasted_iota(jnp.int32, (tall, count), 0)
        row_hit = at == row
        col_hit = jnp.where(at == col, 1.0, 0.0).astype(jnp.bfloat16)
        col_hit = jnp.concatenate(
            [col_hit, jnp.zeros((wide - tall, count), jnp.bfloat16)], axis=0
        )
        x_high = x.astype(jnp.bfloat16).astype(jnp.float32)
        y_high = y.astype(jnp.bfloat16).astype(jnp.float32)
        picked = jnp.concatenate(
            [
                jnp.where(row_hit, part, 0.0).astype(jnp.bfloat16)
                for part in (x_high, x - x_high, y_high, y - y_high, 1.0)
            ],
            axis=0,
        )
        summed = nt_dot(picked, col_hit)
        sum_ref[0] += summed[0:tall] + summed[tall : 2 * tall]
        sum_ref[1] += summed[2 * tall : 3 * tall] + summed[3 * tall : 4 * tall]
        sum_ref[2] += summed[4 * tall :]

    for channel in range(3):
        last = sum_ref[channel, :, pl.ds(side, wide - side)]
        turned = pltpu.roll(last, wide - side - 2 * halo, 1)
        lane = lax.broadcasted_iota(jnp.int32, last.shape, 1)
        sum_ref[channel, :, pl.ds(side, wide - side)] = jnp.where(
            lane < halo, last, jnp.where(lane >= wide - side - halo, turned, 0.0)
        )


def sums_kernel(side, halo, tile_cols, at_ref, ids_ref, points_ref, out_ref, sum_ref):
    vertex_sums(side, halo, tile_cols, at_ref, ids_ref, points_ref, sum_ref)
    out_ref[...] = sum_ref[:, pl.ds(0, out_ref.shape[1]), :]


def relax_kernel(
    side, halo, tile_cols, extent, at_ref, ids_ref, points_ref, mesh_ref, out_ref, sum_ref
):
    vertex_sums(side, halo, tile_cols, at_ref, ids_ref, points_ref, sum_ref)
    span = side + 2 * halo
    wide = sum_ref.shape[2]
    shape = (span, wide)
    row = lax.broadcasted_iota(jnp.int32, shape, 0)
    col = lax.broadcasted_iota(jnp.int32, shape, 1)
    row = jnp.where(row < side + halo, row, row - span) + at_ref[0]
    col = jnp.where(col < side + halo, col, col - wide) + at_ref[1]
    inside = (row >= 0) & (row < extent[0]) & (col >= 0) & (col < extent[1])
    own_pulled = (at_ref[2] == 0).astype(jnp.float32)
    linked = 1.0
    matched = sum_ref[2, pl.ds(0, span), :]
    moving, gains, has, step = [], [], [], []
    for part, pulled in enumerate((own_pulled, 1.0 - own_pulled)):
        gain = mesh_ref[part * 3 + 2]
        diagonal = 4.0 * gain + spring_sec * linked + spring_match * matched * pulled
        gains.append(gain)
        has.append(matched * pulled)
        step.append(jnp.where(inside, relax_rate / diagonal, 0.0))
        moving.append(
            [
                (mesh_ref[part * 3 + c], sum_ref[c, pl.ds(0, span), :] * pulled)
                for c in range(2)
            ]
        )
    for sweep in range(ITERS):
        later = []
        for part in range(2):
            row_of = []
            for c in range(2):
                u, pulled = moving[part][c]
                other = moving[1 - part][c][0]
                laplace = (
                    pltpu.roll(u, 1, 0)
                    + pltpu.roll(u, span - 1, 0)
                    + pltpu.roll(u, 1, 1)
                    + pltpu.roll(u, wide - 1, 1)
                    - 4.0 * u
                )
                force = (
                    gains[part] * laplace
                    + spring_sec * (other - linked * u)
                    + spring_match * (pulled - has[part] * u)
                )
                row_of.append((u + step[part] * force, pulled))
            later.append(row_of)
        moving = later
    for c in range(2):
        out_ref[c] = moving[0][c][0][0:side, 0:side]


def with_halo(value, halo, wide):
    side = value.shape[1]
    after = passed_along(value[:, :halo], "ty", -1)
    before = passed_along(value[:, side - halo :], "ty", 1)
    value = jnp.concatenate([value, after, before], axis=1)
    after = passed_along(value[:, :, :halo], "tx", -1)
    before = passed_along(value[:, :, side - halo :], "tx", 1)
    gap = jnp.zeros(value.shape[:2] + (wide - side - 2 * halo,), value.dtype)
    return jnp.concatenate([value, after, gap, before], axis=2)


def sweeps(moving, gains, sums, at, side, halo, extent):
    sections = lax.axis_size("sec")
    sec_index = at[2]
    has_next = (sec_index < sections - 1).astype(jnp.float32)
    linked = (sec_index > 0).astype(jnp.float32) + has_next
    pulled, matched = sums[0:2] * has_next, sums[2] * has_next
    span, wide = moving.shape[1:]
    row = jnp.arange(span)[:, None]
    col = jnp.arange(wide)[None, :]
    row = jnp.where(row < side + halo, row, row - span) + at[0]
    col = jnp.where(col < side + halo, col, col - wide) + at[1]
    inside = (row >= 0) & (row < extent[0]) & (col >= 0) & (col < extent[1])
    diagonal = 4.0 * gains + spring_sec * linked + spring_match * matched
    step = jnp.where(inside, relax_rate / jnp.where(inside, diagonal, 1.0), 0.0)
    for sweep in range(ITERS):
        lower_sec = passed_along(moving, "sec", 1)
        upper_sec = passed_along(moving, "sec", -1)
        laplace = (
            jnp.roll(moving, 1, 1)
            + jnp.roll(moving, -1, 1)
            + jnp.roll(moving, 1, 2)
            + jnp.roll(moving, -1, 2)
            - 4.0 * moving
        )
        force = (
            gains * laplace
            + spring_sec * (lower_sec + upper_sec - linked * moving)
            + spring_match * (pulled - matched * moving)
        )
        moving = moving + step * force
    return moving[:, :side, :side]


def local_work(lists, counts, blocks):
    total = blocks.shape[0]
    is_live = jnp.arange(lists.shape[1])[None, :] < counts[:, None]
    hit = (lists[:, :, None] == blocks[None, None, :]) & is_live[:, :, None]
    live = jnp.any(hit, axis=1)
    spot = jnp.arange(total)
    rank = jnp.sum(live[:, None, :] & (spot[None, :] < spot[:, None])[None], axis=2)
    taken = live[:, None, :] & (rank[:, None, :] == spot[None, :, None])
    packed = jnp.sum(jnp.where(taken, spot[None, None, :], 0), axis=2)
    number = jnp.sum(live, axis=1)
    return jnp.concatenate([packed, number[:, None]], axis=1).astype(jnp.int32)


def per_device(
    descriptors, positions, vertex_ids, candidate_blocks, candidate_count, displacement, stiffness
):
    point_total, width = descriptors.shape[3:]
    per_tile = point_total // BLK
    tile_rows, tile_cols = lax.axis_size("ty"), lax.axis_size("tx")
    sections = lax.axis_size("sec")
    sec_index = lax.axis_index("sec")
    tiles = tile_rows * tile_cols
    side = displacement.shape[3]
    halo = ITERS
    span = side + 2 * halo
    wide = -(-span // LANES) * LANES
    shares = 2 if sections == 2 and per_tile % 2 == 0 else 1
    part = per_tile // shares
    key_rows = part * BLK

    own_desc = descriptors[0, 0, 0]
    own_place = positions[0, 0, 0].reshape(2, per_tile, BLK)

    def key_part(share):
        blocks = slice(share * part, (share + 1) * part)
        place = own_place[:, blocks].reshape(2 * part, BLK)
        filler = jnp.zeros((PLACE_ROWS - 2 * part, BLK), place.dtype)
        desc = own_desc[share * key_rows : (share + 1) * key_rows]
        return jnp.concatenate([desc, place, filler], axis=0)

    query = jnp.concatenate([own_desc, own_place.reshape(2 * per_tile, BLK)], axis=0)
    whole = jnp.concatenate(
        [vertex_ids[0, 0, 0], candidate_blocks[0, 0, 0], candidate_count[0, 0, 0][None]]
    )
    if shares == 2:
        first = sec_index == 0
        key = jnp.where(first, passed_along(key_part(0), "sec", -1), key_part(1))
        query = jnp.where(first, query, passed_along(query, "sec", 1))
        whole = jnp.where(first, whole, passed_along(whole, "sec", 1))
        share = sec_index
    else:
        key = key_part(0)
        query = passed_along(query, "sec", 1)
        whole = passed_along(whole, "sec", 1)
        share = 0
    keys = spread(key, "tx")
    queries = spread(query, "ty")
    ids = spread(whole[:point_total].reshape(per_tile, LANES), ("ty", "tx"))
    lists = spread(whole[point_total:], "ty")

    key_tile = lax.axis_index("ty") * tile_cols + jnp.arange(tile_cols)
    blocks = (key_tile[:, None] * per_tile + share * part + jnp.arange(part)[None, :]).reshape(-1)
    work = local_work(lists[:, :-1], lists[:, -1], blocks)
    parts = match(work, queries, keys, 16.0 / width, shares, point_total)

    place = query[point_total:].reshape(2, shares, part, LANES)
    place = lax.dynamic_index_in_dim(place, share, 1, keepdims=False).reshape(2 * part, LANES)
    at = jnp.stack(
        [lax.axis_index("ty") * side, lax.axis_index("tx") * side, sec_index]
    ).astype(jnp.int32)
    extent = (side * tile_rows, side * tile_cols)
    own_mesh = jnp.concatenate([displacement[0], stiffness], axis=0)
    sum_shape = pltpu.VMEM((3, -(-span // 16) * 16, wide), jnp.float32)

    if shares == 2:
        other_mesh = lax.ppermute(own_mesh, "sec", [(0, 1), (1, 0)])
        mesh_values = with_halo(jnp.concatenate([own_mesh, other_mesh], axis=0), halo, wide)
        parts = exchanged(parts.reshape((-1,) + parts.shape[2:]), ("sec", "ty"))
        points = exchanged(combine(parts, place, 2 * tiles), ("sec", "ty", "tx"))
        relaxed = pl.pallas_call(
            functools.partial(relax_kernel, side, halo, tile_cols, extent),
            out_shape=jax.ShapeDtypeStruct((2, side, side), jnp.float32),
            in_specs=[in_smem()] + in_vmem(3),
            out_specs=pl.BlockSpec(memory_space=pltpu.VMEM),
            scratch_shapes=[sum_shape],
            compiler_params=pltpu.CompilerParams(vmem_limit_bytes=VMEM_BYTES),
            name="relax",
        )(at, ids, points.reshape(2, tiles, 2 * part, LANES), mesh_values)
        return relaxed[None]

    mesh_values = with_halo(own_mesh, halo, wide)
    parts = exchanged(parts[0], "ty")
    points = passed_along(exchanged(combine(parts, place, tiles), ("ty", "tx")), "sec", -1)
    ids = passed_along(ids, "sec", -1)
    sums = pl.pallas_call(
        functools.partial(sums_kernel, side, halo, tile_cols),
        out_shape=jax.ShapeDtypeStruct((3, span, wide), jnp.float32),
        in_specs=[in_smem()] + in_vmem(2),
        out_specs=pl.BlockSpec(memory_space=pltpu.VMEM),
        scratch_shapes=[sum_shape],
        compiler_params=pltpu.CompilerParams(vmem_limit_bytes=VMEM_BYTES),
        name="sums",
    )(at, ids, points[None])
    return sweeps(mesh_values[0:2], mesh_values[2], sums, at, side, halo, extent)[None]


def solution(mesh):
    in_specs = (
        P("sec", "ty", "tx", None, None),
        P("sec", "ty", "tx", None, None),
        P("sec", "ty", "tx", None),
        P("sec", "ty", "tx", None),
        P("sec", "ty", "tx"),
        P("sec", None, "ty", "tx"),
        P("sec", "ty", "tx"),
    )
    out_specs = P("sec", None, "ty", "tx")
    return jax.shard_map(
        per_device, mesh=mesh, in_specs=in_specs, out_specs=out_specs, check_vma=False
    )
```

profile of v0, /device:TPU:0, one launch (start us, length us, event | category | flops | bytes accessed | tf_op | source)
XLA Modules:
  0.0 119.2 jit_solution(5659899424477902977)
XLA Ops:
  0.7 0.8 concatenate.28
  1.5 4.8 %collective-permute-start = (s32[1057]{0:T(1024)S(1)}, s32[1057]{0:T(1024)S(1)}, u32[]{:S(2)}, u32[]{:S(2)}) collective-permute-start(s32[1057]{0:T(1024)S(1)} %concatenate.28), channel_id=1, source_target_pairs={{0,16},{1,17},{2,18},{3,19},{4,20},{5,21},{6,22},{7,23},{8,24},{9,... | collective-permute-start | bytes 12692 | tf_op jit(solution)/shard_map/ppermute | solution.py:25
  6.3 0.7 reshape_reshape_squeeze.3
  7.0 1.0 pad_maximum_fusion.2
  8.0 1.3 %collective-permute-start.1 = (bf16[1040,128]{1,0:T(8,128)(2,1)S(1)}, bf16[1040,128]{1,0:T(8,128)(2,1)S(1)}, u32[]{:S(2)}, u32[]{:S(2)}) collective-permute-start(bf16[1040,128]{1,0:T(8,128)(2,1)S(1)} %pad_maximum_fusion.2), channel_id=1, source_target_pairs={{0,16},{1,17},{2,18},{3,19},{4,20},{5,21},{6,22},{7,23},{8,24},{9,... | collective-permute-start | bytes 798728 | tf_op jit(solution)/shard_map/ppermute | solution.py:25
  9.3 1.0 slice_bitcast_fusion
  10.5 1.3 %collective-permute-start.2 = (bf16[528,128]{1,0:T(8,128)(2,1)S(1)}, bf16[528,128]{1,0:T(8,128)(2,1)S(1)}, u32[]{:S(2)}, u32[]{:S(2)}) collective-permute-start(bf16[528,128]{1,0:T(8,128)(2,1)S(1)} %maximum_maximum_fusion), channel_id=1, source_target_pairs={{16,0},{17,1},{18,2},{19,3},{20,4},{21,5},{22,6},{23,7},{24,8},{25... | collective-permute-start | bytes 405512 | tf_op jit(solution)/shard_map/ppermute | solution.py:25
  11.9 2.7 %collective-permute-start.3 = (f32[3,128,128]{2,1,0:T(8,128)S(1)}, f32[3,128,128]{2,1,0:T(8,128)S(1)}, u32[]{:S(2)}, u32[]{:S(2)}) collective-permute-start(f32[3,128,128]{2,1,0:T(8,128)S(1)} %pad_maximum_fusion.3), channel_id=1, source_target_pairs={{0,16},{16,0},{1,17},{17,1},{2,18},{18,2},{3,19},{19,3},{4,20},{20... | collective-permute-start | bytes 589832 | tf_op jit(solution)/shard_map/ppermute | solution.py:399
  14.8 0.6 broadcast_in_dim.26
  15.4 3.2 %all-to-all-start.1 = ((s32[4,1,33]{2,1,0:T(1,128)}), s32[4,1,33]{2,1,0:T(1,128)S(1)}, u32[]{:S(2)}, u32[]{:S(2)}) async-start(s32[4,1,33]{2,1,0:T(1,128)} %broadcast_in_dim.26), calls=%async_computation.1 | async-start | bytes 4096 | tf_op jit(solution)/shard_map/all_to_all | solution.py:29
  19.1 3.1 %all-to-all-done.1 = s32[4,1,33]{2,1,0:T(1,128)S(1)} async-done(((s32[4,1,33]{2,1,0:T(1,128)}), s32[4,1,33]{2,1,0:T(1,128)S(1)}, u32[]{:S(2)}, u32[]{:S(2)}) %all-to-all-start.1) | async-done | bytes 560 | tf_op jit(solution)/shard_map/all_to_all | solution.py:29
  22.2 0.9 broadcast_in_dim.31
  23.1 4.9 %all-to-all-start.3 = ((bf16[4,528,128]{2,1,0:T(8,128)(2,1)}), bf16[4,528,128]{2,1,0:T(8,128)(2,1)S(1)}, u32[]{:S(2)}, u32[]{:S(2)}) async-start(bf16[4,528,128]{2,1,0:T(8,128)(2,1)} %broadcast_in_dim.31), calls=%async_computation.3 | async-start | bytes 1081344 | tf_op jit(solution)/shard_map/all_to_all | solution.py:29
  28.3 14.5 %all-to-all-done.3.key_ref = bf16[4,528,128]{2,1,0:T(8,128)(2,1)S(1)} async-done(((bf16[4,528,128]{2,1,0:T(8,128)(2,1)}), bf16[4,528,128]{2,1,0:T(8,128)(2,1)S(1)}, u32[]{:S(2)}, u32[]{:S(2)}) %all-to-all-start.3) | async-done | bytes 540704 | tf_op jit(solution)/shard_map/all_to_all | solution.py:29
  42.8 1.1 broadcast_in_dim.30
  43.9 3.5 %all-to-all-start.2 = ((bf16[4,1040,128]{2,1,0:T(8,128)(2,1)}), bf16[4,1040,128]{2,1,0:T(8,128)(2,1)S(1)}, u32[]{:S(2)}, u32[]{:S(2)}) async-start(bf16[4,1040,128]{2,1,0:T(8,128)(2,1)} %broadcast_in_dim.30), calls=%async_computation.2 | async-start | bytes 2129920 | tf_op jit(solution)/shard_map/all_to_all | solution.py:29
  48.4 2.4 %collective-permute-start.5 = (f32[6,4,128]{2,1,0:T(4,128)S(1)}, f32[6,4,128]{2,1,0:T(4,128)S(1)}, u32[]{:S(2)}, u32[]{:S(2)}) collective-permute-start(f32[6,4,128]{2,1,0:T(4,128)S(1)} %get-tuple-element.8), channel_id=1, source_target_pairs={{0,4},{4,8},{8,12},{1,5},{5,9},{9,13},{2,6},{6,10},{10,14},{3,7},{... | collective-permute-start | bytes 36872 | tf_op jit(solution)/shard_map/ppermute | solution.py:25
  50.7 1.3 %collective-permute-start.4 = (f32[6,4,128]{2,1,0:T(4,128)S(1)}, f32[6,4,128]{2,1,0:T(4,128)S(1)}, u32[]{:S(2)}, u32[]{:S(2)}) collective-permute-start(f32[6,4,128]{2,1,0:T(4,128)S(1)} %get-tuple-element.7), channel_id=1, source_target_pairs={{4,0},{8,4},{12,8},{5,1},{9,5},{13,9},{6,2},{10,6},{14,10},{7,3},{... | collective-permute-start | bytes 36872 | tf_op jit(solution)/shard_map/ppermute | solution.py:25
  52.0 10.0 %all-to-all-done.2.query_ref = bf16[4,1040,128]{2,1,0:T(8,128)(2,1)S(1)} async-done(((bf16[4,1040,128]{2,1,0:T(8,128)(2,1)}), bf16[4,1040,128]{2,1,0:T(8,128)(2,1)S(1)}, u32[]{:S(2)}, u32[]{:S(2)}) %all-to-all-start.2) | async-done | bytes 1064992 | tf_op jit(solution)/shard_map/all_to_all | solution.py:29
  62.0 6.5 %match.1 = f32[2,4,16,128]{3,2,1,0:T(8,128)} custom-call(s32[4,17]{1,0:T(4,128)S(1)} %pad_add_fusion.work_ref, bf16[4,1040,128]{2,1,0:T(8,128)(2,1)S(1)} %all-to-all-done.2.query_ref, bf16[4,528,128]{2,1,0:T(8,128)(2,1)S(1)} %all-to-all-done.3.key_ref), custom_call_target="tpu_custom_call" | custom-call | flops 1073741824 | bytes 1605632 | tf_op jit(solution)/shard_map/match/pallas_call | solution.py:123
  68.5 7.0 %all-to-all-start.4 = ((f32[8,16,128]{2,1,0:T(8,128)}), f32[8,16,128]{2,1,0:T(8,128)S(1)}, u32[]{:S(2)}, u32[]{:S(2)}) async-start(f32[8,16,128]{2,1,0:T(8,128)} %bitcast.14), calls=%async_computation.4 | async-start | bytes 131072 | tf_op jit(solution)/shard_map/all_to_all | solution.py:29
  75.5 4.8 %all-to-all-done.4.parts_ref = f32[8,16,128]{2,1,0:T(8,128)S(1)} async-done(((f32[8,16,128]{2,1,0:T(8,128)}), f32[8,16,128]{2,1,0:T(8,128)S(1)}, u32[]{:S(2)}, u32[]{:S(2)}) %all-to-all-start.4) | async-done | bytes 65568 | tf_op jit(solution)/shard_map/all_to_all | solution.py:29
  80.3 0.6 broadcast_in_dim.25
  81.0 4.0 %all-to-all-start = ((s32[16,8,128]{2,1,0:T(8,128)}), s32[16,8,128]{2,1,0:T(8,128)S(1)}, u32[]{:S(2)}, u32[]{:S(2)}) async-start(s32[16,8,128]{2,1,0:T(8,128)} %broadcast_in_dim.25), calls=%async_computation | async-start | bytes 131072 | tf_op jit(solution)/shard_map/all_to_all | solution.py:29
  85.2 3.9 %collective-permute-start.7 = (f32[6,136,4]{2,1,0:T(8,128)S(1)}, f32[6,136,4]{2,1,0:T(8,128)S(1)}, u32[]{:S(2)}, u32[]{:S(2)}) collective-permute-start(f32[6,136,4]{2,1,0:T(8,128)S(1)} %get-tuple-element.6), channel_id=1, source_target_pairs={{0,1},{1,2},{2,3},{4,5},{5,6},{6,7},{8,9},{9,10},{10,11},{12,13},{... | collective-permute-start | bytes 39176 | tf_op jit(solution)/shard_map/ppermute | solution.py:25
  89.1 1.3 %collective-permute-start.6 = (f32[6,136,4]{2,1,0:T(8,128)S(1)}, f32[6,136,4]{2,1,0:T(8,128)S(1)}, u32[]{:S(2)}, u32[]{:S(2)}) collective-permute-start(f32[6,136,4]{2,1,0:T(8,128)S(1)} %get-tuple-element.5), channel_id=1, source_target_pairs={{1,0},{2,1},{3,2},{5,4},{6,5},{7,6},{9,8},{10,9},{11,10},{13,12},{... | collective-permute-start | bytes 39176 | tf_op jit(solution)/shard_map/ppermute | solution.py:25
  90.4 0.6 constant_dynamic-slice_fusion
  91.0 1.5 %combine.1 = f32[32,8,128]{2,1,0:T(8,128)} custom-call(f32[8,16,128]{2,1,0:T(8,128)} %copy-done.3, bf16[8,128]{1,0:T(8,128)(2,1)} %bitcast.44), custom_call_target="tpu_custom_call" | custom-call | tf_op jit(solution)/shard_map/combine/pallas_call | solution.py:156
  92.5 5.7 %all-to-all-start.5 = ((f32[32,8,128]{2,1,0:T(8,128)}), f32[32,8,128]{2,1,0:T(8,128)S(1)}, u32[]{:S(2)}, u32[]{:S(2)}) async-start(f32[32,8,128]{2,1,0:T(8,128)} %combine.1), calls=%async_computation.5 | async-start | bytes 262144 | tf_op jit(solution)/shard_map/all_to_all | solution.py:29
  98.4 4.6 %collective-permute-done.6 = f32[6,136,4]{2,1,0:T(8,128)S(1)} collective-permute-done((f32[6,136,4]{2,1,0:T(8,128)S(1)}, f32[6,136,4]{2,1,0:T(8,128)S(1)}, u32[]{:S(2)}, u32[]{:S(2)}) %collective-permute-start.6) | collective-permute-done | bytes 13088 | tf_op jit(solution)/shard_map/ppermute | solution.py:25
  103.1 4.0 %all-to-all-done.5 = f32[32,8,128]{2,1,0:T(8,128)S(1)} async-done(((f32[32,8,128]{2,1,0:T(8,128)}), f32[32,8,128]{2,1,0:T(8,128)S(1)}, u32[]{:S(2)}, u32[]{:S(2)}) %all-to-all-start.5) | async-done | bytes 131104 | tf_op jit(solution)/shard_map/all_to_all | solution.py:29
  107.1 12.1 %relax.1 = f32[2,128,128]{2,1,0:T(8,128)} custom-call(s32[3]{0:T(128)S(1)} %pad_add_fusion.1.at_ref, s32[16,8,128]{2,1,0:T(8,128)S(1)} %all-to-all-done.ids_ref, f32[2,16,8,128]{3,2,1,0:T(8,128)S(1)} %bitcast.32, f32[6,136,256]{2,1,0:T(8,128)S(1)} %pad_maximum_fusion.mesh_ref), custom_call_target="tpu_custom_call" | custom-call | tf_op jit(solution)/shard_map/relax/pallas_call | solution.py:403
  (49 shorter events, 2.7 us)
Async XLA Ops:
  0.0 10.3 %copy-start.4 = (bf16[1,1,1,2,1024]{4,3,2,1,0:T(2,128)(2,1)S(1)}, bf16[1,1,1,2,1024]{4,3,2,1,0:T(2,128)(2,1)}, u32[]{:S(2)}) copy-start(bf16[1,1,1,2,1024]{4,3,2,1,0:T(2,128)(2,1)} %param.8) | copy-start | bytes 12292
  0.0 11.8 %copy-start.2 = (f32[1,128,128]{2,1,0:T(8,128)S(1)}, f32[1,128,128]{2,1,0:T(8,128)}, u32[]{:S(2)}) copy-start(f32[1,128,128]{2,1,0:T(8,128)} %param.13) | copy-start | bytes 196612
  0.0 11.9 %copy-start.1 = (f32[1,2,128,128]{3,2,1,0:T(8,128)S(1)}, f32[1,2,128,128]{3,2,1,0:T(8,128)}, u32[]{:S(2)}) copy-start(f32[1,2,128,128]{3,2,1,0:T(8,128)} %param.12) | copy-start | bytes 393220
  1.5 13.3 %collective-permute-start = (s32[1057]{0:T(1024)S(1)}, s32[1057]{0:T(1024)S(1)}, u32[]{:S(2)}, u32[]{:S(2)}) collective-permute-start(s32[1057]{0:T(1024)S(1)} %concatenate.28), channel_id=1, source_target_pairs={{0,16},{1,17},{2,18},{3,19},{4,20},{5,21},{6,22},{7,23},{8,24},{9,... | collective-permute-start | bytes 12692 | tf_op jit(solution)/shard_map/ppermute | solution.py:25
  8.0 20.2 %collective-permute-start.1 = (bf16[1040,128]{1,0:T(8,128)(2,1)S(1)}, bf16[1040,128]{1,0:T(8,128)(2,1)S(1)}, u32[]{:S(2)}, u32[]{:S(2)}) collective-permute-start(bf16[1040,128]{1,0:T(8,128)(2,1)S(1)} %pad_maximum_fusion.2), channel_id=1, source_target_pairs={{0,16},{1,17},{2,18},{3,19},{4,20},{5,21},{6,22},{7,23},{8,24},{9,... | collective-permute-start | bytes 798728 | tf_op jit(solution)/shard_map/ppermute | solution.py:25
  10.5 8.4 %collective-permute-start.2 = (bf16[528,128]{1,0:T(8,128)(2,1)S(1)}, bf16[528,128]{1,0:T(8,128)(2,1)S(1)}, u32[]{:S(2)}, u32[]{:S(2)}) collective-permute-start(bf16[528,128]{1,0:T(8,128)(2,1)S(1)} %maximum_maximum_fusion), channel_id=1, source_target_pairs={{16,0},{17,1},{18,2},{19,3},{20,4},{21,5},{22,6},{23,7},{24,8},{25... | collective-permute-start | bytes 405512 | tf_op jit(solution)/shard_map/ppermute | solution.py:25
  11.9 36.4 %collective-permute-start.3 = (f32[3,128,128]{2,1,0:T(8,128)S(1)}, f32[3,128,128]{2,1,0:T(8,128)S(1)}, u32[]{:S(2)}, u32[]{:S(2)}) collective-permute-start(f32[3,128,128]{2,1,0:T(8,128)S(1)} %pad_maximum_fusion.3), channel_id=1, source_target_pairs={{0,16},{16,0},{1,17},{17,1},{2,18},{18,2},{3,19},{19,3},{4,20},{20... | collective-permute-start | bytes 589832 | tf_op jit(solution)/shard_map/ppermute | solution.py:399
  15.4 6.9 %all-to-all-start.1 = ((s32[4,1,33]{2,1,0:T(1,128)}), s32[4,1,33]{2,1,0:T(1,128)S(1)}, u32[]{:S(2)}, u32[]{:S(2)}) async-start(s32[4,1,33]{2,1,0:T(1,128)} %broadcast_in_dim.26), calls=%async_computation.1 | async-start | bytes 4096 | tf_op jit(solution)/shard_map/all_to_all | solution.py:29
  18.9 9.2 %copy-start = (bf16[1,1,1,1024,128]{4,3,2,1,0:T(8,128)(2,1)S(1)}, bf16[1,1,1,1024,128]{4,3,2,1,0:T(8,128)(2,1)}, u32[]{:S(2)}) copy-start(bf16[1,1,1,1024,128]{4,3,2,1,0:T(8,128)(2,1)} %param.7) | copy-start | bytes 786436
  23.1 19.7 %all-to-all-start.3 = ((bf16[4,528,128]{2,1,0:T(8,128)(2,1)}), bf16[4,528,128]{2,1,0:T(8,128)(2,1)S(1)}, u32[]{:S(2)}, u32[]{:S(2)}) async-start(bf16[4,528,128]{2,1,0:T(8,128)(2,1)} %broadcast_in_dim.31), calls=%async_computation.3 | async-start | bytes 1081344 | tf_op jit(solution)/shard_map/all_to_all | solution.py:29
  43.9 18.1 %all-to-all-start.2 = ((bf16[4,1040,128]{2,1,0:T(8,128)(2,1)}), bf16[4,1040,128]{2,1,0:T(8,128)(2,1)S(1)}, u32[]{:S(2)}, u32[]{:S(2)}) async-start(bf16[4,1040,128]{2,1,0:T(8,128)(2,1)} %broadcast_in_dim.30), calls=%async_computation.2 | async-start | bytes 2129920 | tf_op jit(solution)/shard_map/all_to_all | solution.py:29
  48.4 27.1 %collective-permute-start.5 = (f32[6,4,128]{2,1,0:T(4,128)S(1)}, f32[6,4,128]{2,1,0:T(4,128)S(1)}, u32[]{:S(2)}, u32[]{:S(2)}) collective-permute-start(f32[6,4,128]{2,1,0:T(4,128)S(1)} %get-tuple-element.8), channel_id=1, source_target_pairs={{0,4},{4,8},{8,12},{1,5},{5,9},{9,13},{2,6},{6,10},{10,14},{3,7},{... | collective-permute-start | bytes 36872 | tf_op jit(solution)/shard_map/ppermute | solution.py:25
  50.7 24.8 %collective-permute-start.4 = (f32[6,4,128]{2,1,0:T(4,128)S(1)}, f32[6,4,128]{2,1,0:T(4,128)S(1)}, u32[]{:S(2)}, u32[]{:S(2)}) collective-permute-start(f32[6,4,128]{2,1,0:T(4,128)S(1)} %get-tuple-element.7), channel_id=1, source_target_pairs={{4,0},{8,4},{12,8},{5,1},{9,5},{13,9},{6,2},{10,6},{14,10},{7,3},{... | collective-permute-start | bytes 36872 | tf_op jit(solution)/shard_map/ppermute | solution.py:25
  68.5 11.8 %all-to-all-start.4 = ((f32[8,16,128]{2,1,0:T(8,128)}), f32[8,16,128]{2,1,0:T(8,128)S(1)}, u32[]{:S(2)}, u32[]{:S(2)}) async-start(f32[8,16,128]{2,1,0:T(8,128)} %bitcast.14), calls=%async_computation.4 | async-start | bytes 131072 | tf_op jit(solution)/shard_map/all_to_all | solution.py:29
  80.3 10.6 %copy-start.3 = (f32[8,16,128]{2,1,0:T(8,128)}, f32[8,16,128]{2,1,0:T(8,128)S(1)}, u32[]{:S(2)}) copy-start(f32[8,16,128]{2,1,0:T(8,128)S(1)} %all-to-all-done.4.parts_ref) | copy-start | bytes 196612
  81.0 11.5 %all-to-all-start = ((s32[16,8,128]{2,1,0:T(8,128)}), s32[16,8,128]{2,1,0:T(8,128)S(1)}, u32[]{:S(2)}, u32[]{:S(2)}) async-start(s32[16,8,128]{2,1,0:T(8,128)} %broadcast_in_dim.25), calls=%async_computation | async-start | bytes 131072 | tf_op jit(solution)/shard_map/all_to_all | solution.py:29
  85.2 13.2 %collective-permute-start.7 = (f32[6,136,4]{2,1,0:T(8,128)S(1)}, f32[6,136,4]{2,1,0:T(8,128)S(1)}, u32[]{:S(2)}, u32[]{:S(2)}) collective-permute-start(f32[6,136,4]{2,1,0:T(8,128)S(1)} %get-tuple-element.6), channel_id=1, source_target_pairs={{0,1},{1,2},{2,3},{4,5},{5,6},{6,7},{8,9},{9,10},{10,11},{12,13},{... | collective-permute-start | bytes 39176 | tf_op jit(solution)/shard_map/ppermute | solution.py:25
  89.1 13.9 %collective-permute-start.6 = (f32[6,136,4]{2,1,0:T(8,128)S(1)}, f32[6,136,4]{2,1,0:T(8,128)S(1)}, u32[]{:S(2)}, u32[]{:S(2)}) collective-permute-start(f32[6,136,4]{2,1,0:T(8,128)S(1)} %get-tuple-element.5), channel_id=1, source_target_pairs={{1,0},{2,1},{3,2},{5,4},{6,5},{7,6},{9,8},{10,9},{11,10},{13,12},{... | collective-permute-start | bytes 39176 | tf_op jit(solution)/shard_map/ppermute | solution.py:25
  92.5 14.6 %all-to-all-start.5 = ((f32[32,8,128]{2,1,0:T(8,128)}), f32[32,8,128]{2,1,0:T(8,128)S(1)}, u32[]{:S(2)}, u32[]{:S(2)}) async-start(f32[32,8,128]{2,1,0:T(8,128)} %combine.1), calls=%async_computation.5 | async-start | bytes 262144 | tf_op jit(solution)/shard_map/all_to_all | solution.py:29
where the time goes:
time: 121 us; the launch traced here: 119 us
  starting transfers between devices  47.3 us (39%)
  waiting for transfers between devices  41.4 us (34%)
  Pallas kernels  20.1 us (17%)
  local copies, waits for them, and re-layouts  6.99 us (6%)
  other arithmetic  2.53 us (2%)
    all_to_all x6, waiting for transfers between devices, exchanged(): return lax.all_to_all(value, axes, split_axis=0, concat_axis=0, tiled=True)  36.5 us
    all_to_all x6, starting transfers between devices, exchanged(): return lax.all_to_all(value, axes, split_axis=0, concat_axis=0, tiled=True)  28.3 us
    ppermute x7, starting transfers between devices, passed_along(): return lax.ppermute(value, axis, pairs)  16.2 us
    pallas_call x1, Pallas kernels, per_device(): pl.pallas_call(functools.partial(relax_kernel, side, halo, tile_cols, ext...  12.1 us
    pallas_call x1, Pallas kernels, match(): pl.pallas_call(functools.partial(match_kernel, score_factor * math.log2(m...  6.46 us
    ppermute x7, waiting for transfers between devices, passed_along(): return lax.ppermute(value, axis, pairs)  4.92 us
    broadcast_in_dim x5, local copies, waits for them, and re-layouts, spread(): copies = jnp.broadcast_to(value[None], (lax.axis_size(axes),) + value.shape)  3.2 us
    ppermute x1, starting transfers between devices, per_device(): other_mesh = lax.ppermute(own_mesh, 'sec', [(0, 1), (1, 0)])  2.71 us
  transfers between devices with their start and end apart: 14, of which 7 were waited for; matrix products, arithmetic and copies ran while one was open for 7% of the time, Pallas kernels for 7%

commit v1 on v0

--- a/solution.py
+++ b/solution.py
@@ -46,19 +46,21 @@
     return pl.BlockSpec(memory_space=pltpu.SMEM)
 
 
-def match_kernel(scale, work_ref, query_ref, key_ref, out_ref, place_buf):
+def match_kernel(scale, key_tiles, work_ref, query_ref, *refs):
+    key_refs, (out_ref, key_buf, place_buf) = refs[:key_tiles], refs[key_tiles:]
     shares, tile_rows, out_rows, _ = out_ref.shape
     rows = out_rows // 4
     point_total = shares * rows * LANES
-    key_tiles = key_ref.shape[0]
-    key_rows = key_ref.shape[1] - PLACE_ROWS
+    width = key_buf.shape[2]
+    key_rows = key_buf.shape[1]
     part = key_rows // BLK
     total = key_tiles * part
     step = 256 if point_total % 256 == 0 else LANES
 
     row_at = lax.broadcasted_iota(jnp.int32, (PLACE_ROWS, LANES), 0)
-    for tile in range(key_tiles):
-        place = key_ref[tile, pl.ds(key_rows, PLACE_ROWS), :].astype(jnp.float32)
+    for tile, key_ref in enumerate(key_refs):
+        key_buf[tile] = key_ref[pl.ds(0, key_rows), :]
+        place = key_ref[pl.ds(key_rows, PLACE_ROWS), :].astype(jnp.float32)
         for j in range(part):
             x, y = place[j : j + 1, :], place[part + j : part + j + 1, :]
             stacked = jnp.where(
@@ -77,15 +79,15 @@
 
             def keys_of(block):
                 at = pl.multiple_of(lax.rem(block, part) * BLK, BLK)
-                return key_ref[lax.div(block, part), pl.ds(at, BLK), :]
+                return key_buf[lax.div(block, part), pl.ds(at, BLK), :]
 
             keys = jnp.concatenate([keys_of(first), keys_of(second)], axis=0)
             kept = jnp.where(live, 1.0, 0.0).astype(jnp.bfloat16)
             place = jnp.concatenate([place_buf[first], place_buf[second] * kept], axis=1)
             new_tops, new_sums = [], []
             for c in range(point_total // step):
-                queries = query_ref[tile, pl.ds(c * step, step), :]
-                scores = nt_dot(keys, queries) * scale
+                queries = query_ref[tile, pl.ds(0, width), pl.ds(c * step, step)]
+                scores = jnp.dot(keys, queries, preferred_element_type=jnp.float32) * scale
                 top = jnp.maximum(tops[c], jnp.max(scores, axis=0, keepdims=True))
                 weights = jnp.exp2(scores - top).astype(jnp.bfloat16)
                 added = jnp.dot(place, weights, preferred_element_type=jnp.float32)
@@ -115,25 +117,28 @@
 
 def match(work, queries, keys, score_factor, shares, point_total):
     tile_rows = queries.shape[0]
-    width = queries.shape[2]
-    key_tiles = keys.shape[0]
-    part = (keys.shape[1] - PLACE_ROWS) // BLK
+    key_tiles = len(keys)
+    key_rows, width = keys[0].shape[0] - PLACE_ROWS, keys[0].shape[1]
+    part = key_rows // BLK
     rows = point_total // LANES // shares
     pairs = tile_rows * key_tiles * part
     return pl.pallas_call(
-        functools.partial(match_kernel, score_factor * math.log2(math.e)),
+        functools.partial(match_kernel, score_factor * math.log2(math.e), key_tiles),
         out_shape=jax.ShapeDtypeStruct((shares, tile_rows, 4 * rows, LANES), jnp.float32),
-        in_specs=[in_smem()] + in_vmem(2),
+        in_specs=[in_smem()] + in_vmem(1 + key_tiles),
         out_specs=pl.BlockSpec(memory_space=pltpu.VMEM),
-        scratch_shapes=[pltpu.VMEM((key_tiles * part, PLACE_ROWS, LANES), jnp.bfloat16)],
+        scratch_shapes=[
+            pltpu.VMEM((key_tiles, key_rows, width), jnp.bfloat16),
+            pltpu.VMEM((key_tiles * part, PLACE_ROWS, LANES), jnp.bfloat16),
+        ],
         compiler_params=pltpu.CompilerParams(vmem_limit_bytes=VMEM_BYTES),
         cost_estimate=pl.CostEstimate(
             flops=pairs * point_total * BLK * width,
-            bytes_accessed=2 * (queries.size + keys.size),
+            bytes_accessed=2 * (queries.size + key_tiles * keys[0].size),
             transcendentals=pairs * point_total * BLK // 4,
         ),
         name="match",
-    )(work, queries, keys)
+    )(work, queries, *keys)
 
 
 def combine_kernel(parts_ref, place_ref, out_ref):
@@ -158,75 +163,104 @@
         out_shape=jax.ShapeDtypeStruct((copies,) + place.shape, jnp.float32),
         in_specs=in_vmem(2),
         out_specs=pl.BlockSpec(memory_space=pltpu.VMEM),
+        compiler_params=pltpu.CompilerParams(vmem_limit_bytes=VMEM_BYTES),
         name="combine",
     )(parts, place)
 
 
-def vertex_sums(side, halo, tile_cols, at_ref, ids_ref, points_ref, sum_ref):
+def spots_kernel(side, halo, tile_cols, at_ref, ids_ref, row_ref, col_ref, count_ref):
+    tiles, tall, count = row_ref.shape
+    wide = col_ref.shape[2]
     span = side + 2 * halo
-    tall = -(-span // 16) * 16
-    wide = sum_ref.shape[2]
-    shares, tiles, both_rows, _ = points_ref.shape
-    rows = both_rows // 2
-    along = functools.partial(jnp.concatenate, axis=1)
-
-    def folded(at):
+
+    def folded(at, length):
         return jnp.where(
-            (at >= 0) & (at < side + halo), at, jnp.where((at < 0) & (at >= -halo), at + span, -1)
-        )
-
-    sum_ref[...] = jnp.zeros_like(sum_ref)
+            (at >= 0) & (at < side + halo), at, jnp.where((at < 0) & (at >= -halo), at + length, -1)
+        )
+
+    count_ref[...] = jnp.zeros_like(count_ref)
 
     @pl.loop(0, tiles)
     def _(tile):
         ids = ids_ref[tile]
         tile_of = lax.div(ids, side * side)
         within = lax.rem(ids, side * side)
-        row = folded(lax.div(tile_of, tile_cols) * side + lax.div(within, side) - at_ref[0])
-        col = folded(lax.rem(tile_of, tile_cols) * side + lax.rem(within, side) - at_ref[1])
+        row = lax.div(tile_of, tile_cols) * side + lax.div(within, side) - at_ref[0]
+        col = lax.rem(tile_of, tile_cols) * side + lax.rem(within, side) - at_ref[1]
+        row, col = folded(row, span), folded(col, wide)
+        for i in range(count // LANES):
+            here = slice(i * LANES, (i + 1) * LANES)
+            at = lax.broadcasted_iota(jnp.int32, (tall, LANES), 0)
+            row_ref[tile, :, here] = jnp.where(at == row[i : i + 1, :], 1.0, 0.0).astype(jnp.bfloat16)
+            turned = jnp.broadcast_to(col[i : i + 1, :].astype(jnp.float32), (LANES, LANES)).T
+            at = lax.broadcasted_iota(jnp.int32, (LANES, LANES), 1)
+            for j in range(wide // LANES):
+                lane = (at + j * LANES).astype(jnp.float32)
+                col_ref[tile, here, pl.ds(j * LANES, LANES)] = jnp.where(
+                    turned == lane, 1.0, 0.0
+                ).astype(jnp.bfloat16)
+        count_ref[...] += jnp.dot(
+            row_ref[tile], col_ref[tile], preferred_element_type=jnp.float32
+        )
+
+
+def spots(side, halo, tile_cols, wide, at, ids):
+    tiles = ids.shape[0]
+    count = ids.shape[1] * ids.shape[2]
+    tall = -(-(side + 2 * halo) // 16) * 16
+    return pl.pallas_call(
+        functools.partial(spots_kernel, side, halo, tile_cols),
+        out_shape=(
+            jax.ShapeDtypeStruct((tiles, tall, count), jnp.bfloat16),
+            jax.ShapeDtypeStruct((tiles, count, wide), jnp.bfloat16),
+            jax.ShapeDtypeStruct((tall, wide), jnp.float32),
+        ),
+        in_specs=[in_smem()] + in_vmem(1),
+        out_specs=(pl.BlockSpec(memory_space=pltpu.VMEM),) * 3,
+        compiler_params=pltpu.CompilerParams(vmem_limit_bytes=VMEM_BYTES),
+        cost_estimate=pl.CostEstimate(
+            flops=2 * tiles * tall * count * wide,
+            bytes_accessed=2 * tiles * count * (tall + wide),
+            transcendentals=0,
+        ),
+        name="spots",
+    )(at, ids)
+
+
+def vertex_sums(row_ref, col_ref, points_ref, sum_ref):
+    tall = row_ref.shape[1]
+    shares, tiles, both_rows, _ = points_ref.shape
+    rows = both_rows // 2
+    along = functools.partial(jnp.concatenate, axis=1)
+    sum_ref[...] = jnp.zeros_like(sum_ref)
+
+    @pl.loop(0, tiles)
+    def _(tile):
         values = [points_ref[share, tile] for share in range(shares)]
         x = along([v[i : i + 1, :] for v in values for i in range(rows)])
         y = along([v[i : i + 1, :] for v in values for i in range(rows, 2 * rows)])
-        row, col = (along([v[i : i + 1, :] for i in range(shares * rows)]) for v in (row, col))
-        count = row.shape[1]
-        at = lax.broadcasted_iota(jnp.int32, (tall, count), 0)
-        row_hit = at == row
-        col_hit = jnp.where(at == col, 1.0, 0.0).astype(jnp.bfloat16)
-        col_hit = jnp.concatenate(
-            [col_hit, jnp.zeros((wide - tall, count), jnp.bfloat16)], axis=0
-        )
-        x_high = x.astype(jnp.bfloat16).astype(jnp.float32)
-        y_high = y.astype(jnp.bfloat16).astype(jnp.float32)
-        picked = jnp.concatenate(
-            [
-                jnp.where(row_hit, part, 0.0).astype(jnp.bfloat16)
-                for part in (x_high, x - x_high, y_high, y - y_high, 1.0)
-            ],
-            axis=0,
-        )
-        summed = nt_dot(picked, col_hit)
+        hit = row_ref[tile]
+        parts = []
+        for value in (x, y):
+            high = value.astype(jnp.bfloat16)
+            low = (value - high.astype(jnp.float32)).astype(jnp.bfloat16)
+            parts += [hit * high, hit * low]
+        summed = jnp.dot(
+            jnp.concatenate(parts, axis=0), col_ref[tile], preferred_element_type=jnp.float32
+        )
         sum_ref[0] += summed[0:tall] + summed[tall : 2 * tall]
-        sum_ref[1] += summed[2 * tall : 3 * tall] + summed[3 * tall : 4 * tall]
-        sum_ref[2] += summed[4 * tall :]
-
-    for channel in range(3):
-        last = sum_ref[channel, :, pl.ds(side, wide - side)]
-        turned = pltpu.roll(last, wide - side - 2 * halo, 1)
-        lane = lax.broadcasted_iota(jnp.int32, last.shape, 1)
-        sum_ref[channel, :, pl.ds(side, wide - side)] = jnp.where(
-            lane < halo, last, jnp.where(lane >= wide - side - halo, turned, 0.0)
-        )
-
-
-def sums_kernel(side, halo, tile_cols, at_ref, ids_ref, points_ref, out_ref, sum_ref):
-    vertex_sums(side, halo, tile_cols, at_ref, ids_ref, points_ref, sum_ref)
+        sum_ref[1] += summed[2 * tall : 3 * tall] + summed[3 * tall :]
+
+
+def sums_kernel(row_ref, col_ref, points_ref, out_ref, sum_ref):
+    vertex_sums(row_ref, col_ref, points_ref, sum_ref)
     out_ref[...] = sum_ref[:, pl.ds(0, out_ref.shape[1]), :]
 
 
 def relax_kernel(
-    side, halo, tile_cols, extent, at_ref, ids_ref, points_ref, mesh_ref, out_ref, sum_ref
+    side, halo, extent, at_ref, row_ref, col_ref, count_ref, points_ref, mesh_ref, out_ref, sum_ref
 ):
-    vertex_sums(side, halo, tile_cols, at_ref, ids_ref, points_ref, sum_ref)
+    vertex_sums(row_ref, col_ref, points_ref, sum_ref)
     span = side + 2 * halo
     wide = sum_ref.shape[2]
     shape = (span, wide)
@@ -237,7 +271,7 @@
     inside = (row >= 0) & (row < extent[0]) & (col >= 0) & (col < extent[1])
     own_pulled = (at_ref[2] == 0).astype(jnp.float32)
     linked = 1.0
-    matched = sum_ref[2, pl.ds(0, span), :]
+    matched = count_ref[pl.ds(0, span), :]
     moving, gains, has, step = [], [], [], []
     for part, pulled in enumerate((own_pulled, 1.0 - own_pulled)):
         gain = mesh_ref[part * 3 + 2]
@@ -288,12 +322,12 @@
     return jnp.concatenate([value, after, gap, before], axis=2)
 
 
-def sweeps(moving, gains, sums, at, side, halo, extent):
+def sweeps(moving, gains, sums, number, at, side, halo, extent):
     sections = lax.axis_size("sec")
     sec_index = at[2]
     has_next = (sec_index < sections - 1).astype(jnp.float32)
     linked = (sec_index > 0).astype(jnp.float32) + has_next
-    pulled, matched = sums[0:2] * has_next, sums[2] * has_next
+    pulled, matched = sums * has_next, number * has_next
     span, wide = moving.shape[1:]
     row = jnp.arange(span)[:, None]
     col = jnp.arange(wide)[None, :]
@@ -361,70 +395,83 @@
         desc = own_desc[share * key_rows : (share + 1) * key_rows]
         return jnp.concatenate([desc, place, filler], axis=0)
 
-    query = jnp.concatenate([own_desc, own_place.reshape(2 * per_tile, BLK)], axis=0)
+    filler = jnp.zeros((PLACE_ROWS - 2, point_total), own_desc.dtype)
+    query = jnp.concatenate([own_desc.T, positions[0, 0, 0], filler], axis=0)
     whole = jnp.concatenate(
         [vertex_ids[0, 0, 0], candidate_blocks[0, 0, 0], candidate_count[0, 0, 0][None]]
     )
+    whole = jnp.pad(whole, (0, -whole.shape[0] % (8 * LANES))).reshape(-1, LANES)
     if shares == 2:
         first = sec_index == 0
         key = jnp.where(first, passed_along(key_part(0), "sec", -1), key_part(1))
         query = jnp.where(first, query, passed_along(query, "sec", 1))
-        whole = jnp.where(first, whole, passed_along(whole, "sec", 1))
+        whole = spread(whole, ("sec", "ty", "tx"))[:tiles]
         share = sec_index
     else:
         key = key_part(0)
         query = passed_along(query, "sec", 1)
-        whole = passed_along(whole, "sec", 1)
+        whole = spread(passed_along(whole, "sec", 1), ("ty", "tx"))
         share = 0
-    keys = spread(key, "tx")
+    keys = [key]
+    for j in range(1, tile_cols):
+        turn = [(i, (i + j) % tile_cols) for i in range(tile_cols)]
+        keys.append(lax.ppermute(key, "tx", turn))
     queries = spread(query, "ty")
-    ids = spread(whole[:point_total].reshape(per_tile, LANES), ("ty", "tx"))
-    lists = spread(whole[point_total:], "ty")
-
-    key_tile = lax.axis_index("ty") * tile_cols + jnp.arange(tile_cols)
+
+    ids = whole[:, :per_tile]
+    lists = whole[:, per_tile:].reshape(tile_rows, tile_cols, -1)
+    lists = lax.dynamic_index_in_dim(lists, lax.axis_index("tx"), 1, keepdims=False)
+    cand = candidate_blocks.shape[3]
+    key_tile = lax.axis_index("ty") * tile_cols + jnp.mod(
+        lax.axis_index("tx") - jnp.arange(tile_cols), tile_cols
+    )
     blocks = (key_tile[:, None] * per_tile + share * part + jnp.arange(part)[None, :]).reshape(-1)
-    work = local_work(lists[:, :-1], lists[:, -1], blocks)
-    parts = match(work, queries, keys, 16.0 / width, shares, point_total)
-
-    place = query[point_total:].reshape(2, shares, part, LANES)
+    work = local_work(lists[:, :cand], lists[:, cand], blocks)
+
+    place = query[width : width + 2].reshape(2, shares, part, LANES)
     place = lax.dynamic_index_in_dim(place, share, 1, keepdims=False).reshape(2 * part, LANES)
     at = jnp.stack(
         [lax.axis_index("ty") * side, lax.axis_index("tx") * side, sec_index]
     ).astype(jnp.int32)
     extent = (side * tile_rows, side * tile_cols)
     own_mesh = jnp.concatenate([displacement[0], stiffness], axis=0)
-    sum_shape = pltpu.VMEM((3, -(-span // 16) * 16, wide), jnp.float32)
+    sum_shape = pltpu.VMEM((2, -(-span // 16) * 16, wide), jnp.float32)
 
     if shares == 2:
+        row_hit, col_hit, number = spots(side, halo, tile_cols, wide, at, ids)
         other_mesh = lax.ppermute(own_mesh, "sec", [(0, 1), (1, 0)])
         mesh_values = with_halo(jnp.concatenate([own_mesh, other_mesh], axis=0), halo, wide)
+        parts = match(work, queries, keys, 16.0 / width, shares, point_total)
         parts = exchanged(parts.reshape((-1,) + parts.shape[2:]), ("sec", "ty"))
         points = exchanged(combine(parts, place, 2 * tiles), ("sec", "ty", "tx"))
         relaxed = pl.pallas_call(
-            functools.partial(relax_kernel, side, halo, tile_cols, extent),
+            functools.partial(relax_kernel, side, halo, extent),
             out_shape=jax.ShapeDtypeStruct((2, side, side), jnp.float32),
-            in_specs=[in_smem()] + in_vmem(3),
+            in_specs=[in_smem()] + in_vmem(5),
             out_specs=pl.BlockSpec(memory_space=pltpu.VMEM),
             scratch_shapes=[sum_shape],
             compiler_params=pltpu.CompilerParams(vmem_limit_bytes=VMEM_BYTES),
             name="relax",
-        )(at, ids, points.reshape(2, tiles, 2 * part, LANES), mesh_values)
+        )(at, row_hit, col_hit, number, points.reshape(2, tiles, 2 * part, LANES), mesh_values)
         return relaxed[None]
 
+    ids = passed_along(ids, "sec", -1)
+    row_hit, col_hit, number = spots(side, halo, tile_cols, wide, at, ids)
     mesh_values = with_halo(own_mesh, halo, wide)
+    parts = match(work, queries, keys, 16.0 / width, shares, point_total)
     parts = exchanged(parts[0], "ty")
     points = passed_along(exchanged(combine(parts, place, tiles), ("ty", "tx")), "sec", -1)
-    ids = passed_along(ids, "sec", -1)
     sums = pl.pallas_call(
-        functools.partial(sums_kernel, side, halo, tile_cols),
-        out_shape=jax.ShapeDtypeStruct((3, span, wide), jnp.float32),
-        in_specs=[in_smem()] + in_vmem(2),
+        sums_kernel,
+        out_shape=jax.ShapeDtypeStruct((2, span, wide), jnp.float32),
+        in_specs=in_vmem(3),
         out_specs=pl.BlockSpec(memory_space=pltpu.VMEM),
         scratch_shapes=[sum_shape],
         compiler_params=pltpu.CompilerParams(vmem_limit_bytes=VMEM_BYTES),
         name="sums",
-    )(at, ids, points[None])
-    return sweeps(mesh_values[0:2], mesh_values[2], sums, at, side, halo, extent)[None]
+    )(row_hit, col_hit, points[None])
+    moving, gains = mesh_values[0:2], mesh_values[2]
+    return sweeps(moving, gains, sums, number[:span], at, side, halo, extent)[None]
 
 
 def solution(mesh):

time: 121 us -> 114 us (0.942)
  waiting for transfers between devices: 41.4 us -> 19.3 us
  local copies, waits for them, and re-layouts: 6.99 us -> 18.5 us
  Pallas kernels: 20.1 us -> 25.3 us
  starting transfers between devices: 47.3 us -> 42.6 us
  other arithmetic: 2.53 us -> 6.58 us
    all_to_all x6 -> x4, waiting for transfers between devices: 36.5 us -> 19.2 us  [exchanged(): return lax.all_to_all(value, axes, split_axis=0, concat_axis=0, tiled=True)]
    unnamed x11 -> x16, local copies, waits for them, and re-layouts: 0.02 us -> 12 us
    all_to_all x6 -> x4, starting transfers between devices: 28.3 us -> 17.7 us  [exchanged(): return lax.all_to_all(value, axes, split_axis=0, concat_axis=0, tiled=True)]
    pallas_call x1 -> x2, Pallas kernels: 12.1 us -> 18.4 us  [the longest x1 10.3 us: per_device(): pl.pallas_call(functools.partial(relax_kernel, side, halo, extent), out_s...]
    ppermute x7 -> x6, waiting for transfers between devices: 4.92 us -> 0.02 us  [passed_along(): return lax.ppermute(value, axis, pairs)]
    ppermute x0 -> x3, starting transfers between devices: none -> 4.75 us  [per_device(): keys.append(lax.ppermute(key, 'tx', turn))]
    broadcast_in_dim x5 -> x3, local copies, waits for them, and re-layouts: 3.2 us -> 1.92 us  [spread(): copies = jnp.broadcast_to(value[None], (lax.axis_size(axes),) + value.shape)]
    ppermute x7 -> x6, starting transfers between devices: 16.2 us -> 17.2 us  [passed_along(): return lax.ppermute(value, axis, pairs)]
  transfers between devices with their start and end apart: 14 -> 14, of which waited for: 7 -> 2; matrix products, arithmetic and copies ran while one was open for 7% -> 11% of each run, Pallas kernels for 7% -> 13%
where the time goes in v1:
time: 114 us; the launch traced here: 113 us
  starting transfers between devices  42.6 us (37%)
  Pallas kernels  25.3 us (22%)
  waiting for transfers between devices  19.3 us (17%)
  local copies, waits for them, and re-layouts  18.5 us (16%)
  other arithmetic  6.58 us (6%)
    all_to_all x4, waiting for transfers between devices, exchanged(): return lax.all_to_all(value, axes, split_axis=0, concat_axis=0, tiled=True)  19.2 us
    all_to_all x4, starting transfers between devices, exchanged(): return lax.all_to_all(value, axes, split_axis=0, concat_axis=0, tiled=True)  17.7 us
    ppermute x6, starting transfers between devices, passed_along(): return lax.ppermute(value, axis, pairs)  17.2 us
    unnamed x16, local copies, waits for them, and re-layouts  12 us
    pallas_call x1, Pallas kernels, per_device(): pl.pallas_call(functools.partial(relax_kernel, side, halo, extent), out_s...  10.3 us
    pallas_call x1, Pallas kernels, spots(): pl.pallas_call(functools.partial(spots_kernel, side, halo, tile_cols), ou...  8.16 us
    pallas_call x1, Pallas kernels, match(): pl.pallas_call(functools.partial(match_kernel, score_factor * math.log2(m...  6.16 us
    ppermute x3, starting transfers between devices, per_device(): keys.append(lax.ppermute(key, 'tx', turn))  4.75 us
  transfers between devices with their start and end apart: 14, of which 2 were waited for; matrix products, arithmetic and copies ran while one was open for 11% of the time, Pallas kernels for 13%

profile of v1, /device:TPU:0, one launch (start us, length us, event | category | flops | bytes accessed | tf_op | source)
XLA Modules:
  0.0 113.3 jit_solution(5456536941938747815)
XLA Ops:
  0.0 1.0 pad_maximum_fusion.2
  1.0 3.0 %collective-permute-start.5 = (f32[3,128,128]{2,1,0:T(8,128)S(1)}, f32[3,128,128]{2,1,0:T(8,128)S(1)}, u32[]{:S(2)}, u32[]{:S(2)}) collective-permute-start(f32[3,128,128]{2,1,0:T(8,128)S(1)} %pad_maximum_fusion.2), channel_id=1, source_target_pairs={{0,16},{16,0},{1,17},{17,1},{2,18},{18,2},{3,19},{19,3},{4,20},{20... | collective-permute-start | bytes 589832 | tf_op jit(solution)/shard_map/ppermute | solution.py:442
  4.7 0.8 concatenate.28
  6.1 4.9 %all-to-all-start = ((s32[32,16,128]{2,1,0:T(8,128)}), s32[32,16,128]{2,1,0:T(8,128)S(1)}, u32[]{:S(2)}, u32[]{:S(2)}) async-start(s32[32,16,128]{2,1,0:T(8,128)} %broadcast_in_dim.23), calls=%async_computation | async-start | bytes 524288 | tf_op jit(solution)/shard_map/all_to_all | solution.py:29
  11.8 1.0 slice_bitcast_fusion
  13.0 1.3 %collective-permute-start.1 = (bf16[528,128]{1,0:T(8,128)(2,1)S(1)}, bf16[528,128]{1,0:T(8,128)(2,1)S(1)}, u32[]{:S(2)}, u32[]{:S(2)}) collective-permute-start(bf16[528,128]{1,0:T(8,128)(2,1)S(1)} %maximum_maximum_fusion.1), channel_id=1, source_target_pairs={{16,0},{17,1},{18,2},{19,3},{20,4},{21,5},{22,6},{23,7},{24,8},{25... | collective-permute-start | bytes 405512 | tf_op jit(solution)/shard_map/ppermute | solution.py:25
  14.4 0.9 copy.17
  15.3 1.1 maximum_maximum_fusion
  16.4 4.6 %collective-permute-start = (bf16[144,1024]{0,1:T(8,128)(2,1)S(1)}, bf16[144,1024]{0,1:T(8,128)(2,1)S(1)}, u32[]{:S(2)}, u32[]{:S(2)}) collective-permute-start(bf16[144,1024]{0,1:T(8,128)(2,1)S(1)} %maximum_maximum_fusion), channel_id=1, source_target_pairs={{0,16},{1,17},{2,18},{3,19},{4,20},{5,21},{6,22},{7,23},{8,24},{9,... | collective-permute-start | bytes 884744 | tf_op jit(solution)/shard_map/ppermute | solution.py:25
  21.3 0.8 pad_maximum_fusion.5
  22.1 1.3 %collective-permute-start.6 = (f32[6,4,128]{2,1,0:T(4,128)S(1)}, f32[6,4,128]{2,1,0:T(4,128)S(1)}, u32[]{:S(2)}, u32[]{:S(2)}) collective-permute-start(f32[6,4,128]{2,1,0:T(4,128)S(1)} %get-tuple-element.13), channel_id=1, source_target_pairs={{4,0},{8,4},{12,8},{5,1},{9,5},{13,9},{6,2},{10,6},{14,10},{7,3},{... | collective-permute-start | bytes 36872 | tf_op jit(solution)/shard_map/ppermute | solution.py:25
  23.3 3.0 %collective-permute-start.7 = (f32[6,4,128]{2,1,0:T(4,128)S(1)}, f32[6,4,128]{2,1,0:T(4,128)S(1)}, u32[]{:S(2)}, u32[]{:S(2)}) collective-permute-start(f32[6,4,128]{2,1,0:T(4,128)S(1)} %get-tuple-element.14), channel_id=1, source_target_pairs={{0,4},{4,8},{8,12},{1,5},{5,9},{9,13},{2,6},{6,10},{10,14},{3,7},{... | collective-permute-start | bytes 36872 | tf_op jit(solution)/shard_map/ppermute | solution.py:25
  26.5 3.7 %collective-permute-start.4 = (bf16[528,128]{1,0:T(8,128)(2,1)S(1)}, bf16[528,128]{1,0:T(8,128)(2,1)S(1)}, u32[]{:S(2)}, u32[]{:S(2)}) collective-permute-start(bf16[528,128]{1,0:T(8,128)(2,1)S(1)} %maximum_select_fusion.refs_0_), channel_id=1, source_target_pairs={{0,3},{1,0},{2,1},{3,2},{4,7},{5,4},{6,5},{7,6},{8,11},{9,8},{10,9... | collective-permute-start | bytes 405512 | tf_op jit(solution)/shard_map/ppermute | solution.py:418
  30.2 1.1 collective-permute-start.2
  31.3 1.0 pad_maximum_fusion.1
  32.3 1.0 fusion.5
  33.3 1.3 %collective-permute-start.8 = (f32[6,136,4]{2,1,0:T(8,128)}, f32[6,136,4]{2,1,0:T(8,128)}, u32[]{:S(2)}, u32[]{:S(2)}) collective-permute-start(f32[6,136,4]{2,1,0:T(8,128)} %get-tuple-element.11), channel_id=1, source_target_pairs={{1,0},{2,1},{3,2},{5,4},{6,5},{7,6},{9,8},{10,9},{11,10},{13,12},{... | collective-permute-start | bytes 39176 | tf_op jit(solution)/shard_map/ppermute | solution.py:25
  34.6 5.7 %collective-permute-start.9 = (f32[6,136,4]{2,1,0:T(8,128)}, f32[6,136,4]{2,1,0:T(8,128)}, u32[]{:S(2)}, u32[]{:S(2)}) collective-permute-start(f32[6,136,4]{2,1,0:T(8,128)} %get-tuple-element.12), channel_id=1, source_target_pairs={{0,1},{1,2},{2,3},{4,5},{5,6},{6,7},{8,9},{9,10},{10,11},{12,13},{... | collective-permute-start | bytes 39176 | tf_op jit(solution)/shard_map/ppermute | solution.py:25
  40.7 1.2 %broadcast_in_dim.56 = bf16[4,144,1024]{2,1,0:T(8,128)(2,1)} broadcast(bf16[144,1024]{1,0:T(8,128)(2,1)S(1)} %copy.18), dimensions={1,2} | broadcast | bytes 1474560 | tf_op jit(solution)/shard_map/broadcast_in_dim | solution.py:33
  41.9 3.5 %all-to-all-start.1 = ((bf16[4,144,1024]{2,1,0:T(8,128)(2,1)}), bf16[4,144,1024]{2,1,0:T(8,128)(2,1)S(1)}, u32[]{:S(2)}, u32[]{:S(2)}) async-start(bf16[4,144,1024]{2,1,0:T(8,128)(2,1)} %broadcast_in_dim.56), calls=%async_computation.1 | async-start | bytes 2359296 | tf_op jit(solution)/shard_map/all_to_all | solution.py:29
  46.8 14.5 %all-to-all-done.1.query_ref = bf16[4,144,1024]{2,1,0:T(8,128)(2,1)S(1)} async-done(((bf16[4,144,1024]{2,1,0:T(8,128)(2,1)}), bf16[4,144,1024]{2,1,0:T(8,128)(2,1)S(1)}, u32[]{:S(2)}, u32[]{:S(2)}) %all-to-all-start.1) | async-done | bytes 1179680 | tf_op jit(solution)/shard_map/all_to_all | solution.py:29
  61.3 6.2 %match.1 = f32[2,4,16,128]{3,2,1,0:T(8,128)} custom-call(s32[4,17]{1,0:T(4,128)S(1)} %pad_add_fusion.work_ref, bf16[4,144,1024]{2,1,0:T(8,128)(2,1)S(1)} %all-to-all-done.1.query_ref, bf16[528,128]{1,0:T(8,128)(2,1)S(1)} %maximum_select_fusion.refs_0_, bf16[528,128]{1,0:T(8,128)(2,1)S(1)} %collective-permute-done.2.refs_1_, ...), custom_call_target="tpu_custom_call" | custom-call | flops 1073741824 | bytes 1720320 | tf_op jit(solution)/shard_map/match/pallas_call | solution.py:125
  67.5 5.8 %all-to-all-start.2 = ((f32[8,16,128]{2,1,0:T(8,128)}), f32[8,16,128]{2,1,0:T(8,128)S(1)}, u32[]{:S(2)}, u32[]{:S(2)}) async-start(f32[8,16,128]{2,1,0:T(8,128)} %bitcast.17), calls=%async_computation.2 | async-start | bytes 131072 | tf_op jit(solution)/shard_map/all_to_all | solution.py:29
  73.4 4.7 %all-to-all-done.2.parts_ref = f32[8,16,128]{2,1,0:T(8,128)S(1)} async-done(((f32[8,16,128]{2,1,0:T(8,128)}), f32[8,16,128]{2,1,0:T(8,128)S(1)}, u32[]{:S(2)}, u32[]{:S(2)}) %all-to-all-start.2) | async-done | bytes 65568 | tf_op jit(solution)/shard_map/all_to_all | solution.py:29
  78.8 3.5 %all-to-all-start.3 = ((f32[32,8,128]{2,1,0:T(8,128)}), f32[32,8,128]{2,1,0:T(8,128)S(1)}, u32[]{:S(2)}, u32[]{:S(2)}) async-start(f32[32,8,128]{2,1,0:T(8,128)} %combine.1), calls=%async_computation.3 | async-start | bytes 262144 | tf_op jit(solution)/shard_map/all_to_all | solution.py:29
  82.3 1.3 %pad_maximum_fusion.mesh_ref = f32[6,136,256]{2,1,0:T(8,128)S(1)} fusion(f32[6,136,4]{2,1,0:T(8,128)} %collective-permute-done.9, f32[6,136,4]{2,1,0:T(8,128)} %collective-permute-done.8, f32[6,4,128]{2,1,0:T(4,128)S(1)} %collective-permute-done.7, f32[6,4,128]{2,1,0:T(4,128)S(1)} %collective-permute-done.6, f32[3,128,128]{2,1,0:T(8,128)S(1)} %collective-permute-done.5, ...), kind=kLoop, calls=%fused_computation | loop fusion | flops 1462272 | bytes 1280512 | tf_op jit(solution)/shard_map/concatenate | solution.py:322
  83.6 8.2 %spots.1 = (bf16[16,144,1024]{2,1,0:T(8,128)(2,1)S(1)}, bf16[16,1024,256]{2,1,0:T(8,128)(2,1)S(1)}, f32[144,256]{1,0:T(8,128)S(1)}) custom-call(s32[3]{0:T(128)S(1)} %pad_add_fusion.1.at_ref, s32[16,8,128]{2,1,0:T(8,128)S(1)} %get-tuple-element.18.ids_ref), custom_call_target="tpu_custom_call" | custom-call | flops 1207959552 | bytes 13107200 | tf_op jit(solution)/shard_map/spots/pallas_call | solution.py:211
  91.8 3.2 %copy-done = bf16[16,1024,256]{2,1,0:T(8,128)(2,1)} copy-done((bf16[16,1024,256]{2,1,0:T(8,128)(2,1)}, bf16[16,1024,256]{2,1,0:T(8,128)(2,1)S(1)}, u32[]{:S(2)}) %copy-start) | copy-done | bytes 8388632
  95.1 2.2 %copy-done.2 = bf16[16,144,1024]{2,1,0:T(8,128)(2,1)} copy-done((bf16[16,144,1024]{2,1,0:T(8,128)(2,1)}, bf16[16,144,1024]{2,1,0:T(8,128)(2,1)S(1)}, u32[]{:S(2)}) %copy-start.2) | copy-done | bytes 4718616
  97.3 3.4 %copy-done.1 = bf16[16,1024,256]{2,1,0:T(8,128)(2,1)S(1)} copy-done((bf16[16,1024,256]{2,1,0:T(8,128)(2,1)S(1)}, bf16[16,1024,256]{2,1,0:T(8,128)(2,1)}, u32[]{:S(2)}) %copy-start.1) | copy-done | bytes 8388632
  100.7 2.3 %copy-done.3 = bf16[16,144,1024]{2,1,0:T(8,128)(2,1)S(1)} copy-done((bf16[16,144,1024]{2,1,0:T(8,128)(2,1)S(1)}, bf16[16,144,1024]{2,1,0:T(8,128)(2,1)}, u32[]{:S(2)}) %copy-start.3) | copy-done | bytes 4718616
  103.0 10.3 %relax.1 = f32[2,128,128]{2,1,0:T(8,128)} custom-call(s32[3]{0:T(128)S(1)} %pad_add_fusion.1.at_ref, bf16[16,144,1024]{2,1,0:T(8,128)(2,1)S(1)} %copy-done.3, bf16[16,1024,256]{2,1,0:T(8,128)(2,1)S(1)} %copy-done.1, f32[144,256]{1,0:T(8,128)S(1)} %get-tuple-element.10.count_ref, f32[2,16,8,128]{3,2,1,0:T(8,128)S(1)} %bitcast.34, ...), custom_call_target="tpu_custom_call" | custom-call | tf_op jit(solution)/shard_map/relax/pallas_call | solution.py:447
  (60 shorter events, 4.7 us)
Async XLA Ops:
  0.0 40.3 %copy-start.4 = (bf16[1,1,1,1024,128]{4,3,2,1,0:T(8,128)(2,1)S(1)}, bf16[1,1,1,1024,128]{4,3,2,1,0:T(8,128)(2,1)}, u32[]{:S(2)}) copy-start(bf16[1,1,1,1024,128]{4,3,2,1,0:T(8,128)(2,1)} %param.7) | copy-start | bytes 786436
  1.0 20.3 %collective-permute-start.5 = (f32[3,128,128]{2,1,0:T(8,128)S(1)}, f32[3,128,128]{2,1,0:T(8,128)S(1)}, u32[]{:S(2)}, u32[]{:S(2)}) collective-permute-start(f32[3,128,128]{2,1,0:T(8,128)S(1)} %pad_maximum_fusion.2), channel_id=1, source_target_pairs={{0,16},{16,0},{1,17},{17,1},{2,18},{18,2},{3,19},{19,3},{4,20},{20... | collective-permute-start | bytes 589832 | tf_op jit(solution)/shard_map/ppermute | solution.py:442
  6.1 34.6 %all-to-all-start = ((s32[32,16,128]{2,1,0:T(8,128)}), s32[32,16,128]{2,1,0:T(8,128)S(1)}, u32[]{:S(2)}, u32[]{:S(2)}) async-start(s32[32,16,128]{2,1,0:T(8,128)} %broadcast_in_dim.23), calls=%async_computation | async-start | bytes 524288 | tf_op jit(solution)/shard_map/all_to_all | solution.py:29
  13.0 13.4 %collective-permute-start.1 = (bf16[528,128]{1,0:T(8,128)(2,1)S(1)}, bf16[528,128]{1,0:T(8,128)(2,1)S(1)}, u32[]{:S(2)}, u32[]{:S(2)}) collective-permute-start(bf16[528,128]{1,0:T(8,128)(2,1)S(1)} %maximum_maximum_fusion.1), channel_id=1, source_target_pairs={{16,0},{17,1},{18,2},{19,3},{20,4},{21,5},{22,6},{23,7},{24,8},{25... | collective-permute-start | bytes 405512 | tf_op jit(solution)/shard_map/ppermute | solution.py:25
  16.4 18.2 %collective-permute-start = (bf16[144,1024]{0,1:T(8,128)(2,1)S(1)}, bf16[144,1024]{0,1:T(8,128)(2,1)S(1)}, u32[]{:S(2)}, u32[]{:S(2)}) collective-permute-start(bf16[144,1024]{0,1:T(8,128)(2,1)S(1)} %maximum_maximum_fusion), channel_id=1, source_target_pairs={{0,16},{1,17},{2,18},{3,19},{4,20},{5,21},{6,22},{7,23},{8,24},{9,... | collective-permute-start | bytes 884744 | tf_op jit(solution)/shard_map/ppermute | solution.py:25
  22.1 8.2 %collective-permute-start.6 = (f32[6,4,128]{2,1,0:T(4,128)S(1)}, f32[6,4,128]{2,1,0:T(4,128)S(1)}, u32[]{:S(2)}, u32[]{:S(2)}) collective-permute-start(f32[6,4,128]{2,1,0:T(4,128)S(1)} %get-tuple-element.13), channel_id=1, source_target_pairs={{4,0},{8,4},{12,8},{5,1},{9,5},{13,9},{6,2},{10,6},{14,10},{7,3},{... | collective-permute-start | bytes 36872 | tf_op jit(solution)/shard_map/ppermute | solution.py:25
  23.3 8.0 %collective-permute-start.7 = (f32[6,4,128]{2,1,0:T(4,128)S(1)}, f32[6,4,128]{2,1,0:T(4,128)S(1)}, u32[]{:S(2)}, u32[]{:S(2)}) collective-permute-start(f32[6,4,128]{2,1,0:T(4,128)S(1)} %get-tuple-element.14), channel_id=1, source_target_pairs={{0,4},{4,8},{8,12},{1,5},{5,9},{9,13},{2,6},{6,10},{10,14},{3,7},{... | collective-permute-start | bytes 36872 | tf_op jit(solution)/shard_map/ppermute | solution.py:25
  26.5 20.2 %collective-permute-start.4 = (bf16[528,128]{1,0:T(8,128)(2,1)S(1)}, bf16[528,128]{1,0:T(8,128)(2,1)S(1)}, u32[]{:S(2)}, u32[]{:S(2)}) collective-permute-start(bf16[528,128]{1,0:T(8,128)(2,1)S(1)} %maximum_select_fusion.refs_0_), channel_id=1, source_target_pairs={{0,3},{1,0},{2,1},{3,2},{4,7},{5,4},{6,5},{7,6},{8,11},{9,8},{10,9... | collective-permute-start | bytes 405512 | tf_op jit(solution)/shard_map/ppermute | solution.py:418
  30.2 16.6 %collective-permute-start.3 = (bf16[528,128]{1,0:T(8,128)(2,1)S(1)}, bf16[528,128]{1,0:T(8,128)(2,1)S(1)}, u32[]{:S(2)}, u32[]{:S(2)}) collective-permute-start(bf16[528,128]{1,0:T(8,128)(2,1)S(1)} %maximum_select_fusion.refs_0_), channel_id=1, source_target_pairs={{0,2},{1,3},{2,0},{3,1},{4,6},{5,7},{6,4},{7,5},{8,10},{9,11},{10,... | collective-permute-start | bytes 405512 | tf_op jit(solution)/shard_map/ppermute | solution.py:418
  30.2 16.6 %collective-permute-start.2 = (bf16[528,128]{1,0:T(8,128)(2,1)S(1)}, bf16[528,128]{1,0:T(8,128)(2,1)S(1)}, u32[]{:S(2)}, u32[]{:S(2)}) collective-permute-start(bf16[528,128]{1,0:T(8,128)(2,1)S(1)} %maximum_select_fusion.refs_0_), channel_id=1, source_target_pairs={{0,1},{1,2},{2,3},{3,0},{4,5},{5,6},{6,7},{7,4},{8,9},{9,10},{10,1... | collective-permute-start | bytes 405512 | tf_op jit(solution)/shard_map/ppermute | solution.py:418
  33.3 49.0 %collective-permute-start.8 = (f32[6,136,4]{2,1,0:T(8,128)}, f32[6,136,4]{2,1,0:T(8,128)}, u32[]{:S(2)}, u32[]{:S(2)}) collective-permute-start(f32[6,136,4]{2,1,0:T(8,128)} %get-tuple-element.11), channel_id=1, source_target_pairs={{1,0},{2,1},{3,2},{5,4},{6,5},{7,6},{9,8},{10,9},{11,10},{13,12},{... | collective-permute-start | bytes 39176 | tf_op jit(solution)/shard_map/ppermute | solution.py:25
  34.6 47.7 %collective-permute-start.9 = (f32[6,136,4]{2,1,0:T(8,128)}, f32[6,136,4]{2,1,0:T(8,128)}, u32[]{:S(2)}, u32[]{:S(2)}) collective-permute-start(f32[6,136,4]{2,1,0:T(8,128)} %get-tuple-element.12), channel_id=1, source_target_pairs={{0,1},{1,2},{2,3},{4,5},{5,6},{6,7},{8,9},{9,10},{10,11},{12,13},{... | collective-permute-start | bytes 39176 | tf_op jit(solution)/shard_map/ppermute | solution.py:25
  40.7 41.6 %copy-start.5 = (f32[1,2,128,128]{3,2,1,0:T(8,128)S(1)}, f32[1,2,128,128]{3,2,1,0:T(8,128)}, u32[]{:S(2)}) copy-start(f32[1,2,128,128]{3,2,1,0:T(8,128)} %param.12) | copy-start | bytes 393220
  40.7 41.6 %copy-start.6 = (f32[1,128,128]{2,1,0:T(8,128)S(1)}, f32[1,128,128]{2,1,0:T(8,128)}, u32[]{:S(2)}) copy-start(f32[1,128,128]{2,1,0:T(8,128)} %param.13) | copy-start | bytes 196612
  41.9 19.4 %all-to-all-start.1 = ((bf16[4,144,1024]{2,1,0:T(8,128)(2,1)}), bf16[4,144,1024]{2,1,0:T(8,128)(2,1)S(1)}, u32[]{:S(2)}, u32[]{:S(2)}) async-start(bf16[4,144,1024]{2,1,0:T(8,128)(2,1)} %broadcast_in_dim.56), calls=%async_computation.1 | async-start | bytes 2359296 | tf_op jit(solution)/shard_map/all_to_all | solution.py:29
  67.5 10.6 %all-to-all-start.2 = ((f32[8,16,128]{2,1,0:T(8,128)}), f32[8,16,128]{2,1,0:T(8,128)S(1)}, u32[]{:S(2)}, u32[]{:S(2)}) async-start(f32[8,16,128]{2,1,0:T(8,128)} %bitcast.17), calls=%async_computation.2 | async-start | bytes 131072 | tf_op jit(solution)/shard_map/all_to_all | solution.py:29
  78.8 18.5 %all-to-all-start.3 = ((f32[32,8,128]{2,1,0:T(8,128)}), f32[32,8,128]{2,1,0:T(8,128)S(1)}, u32[]{:S(2)}, u32[]{:S(2)}) async-start(f32[32,8,128]{2,1,0:T(8,128)} %combine.1), calls=%async_computation.3 | async-start | bytes 262144 | tf_op jit(solution)/shard_map/all_to_all | solution.py:29
  91.8 3.2 %copy-start = (bf16[16,1024,256]{2,1,0:T(8,128)(2,1)}, bf16[16,1024,256]{2,1,0:T(8,128)(2,1)S(1)}, u32[]{:S(2)}) copy-start(bf16[16,1024,256]{2,1,0:T(8,128)(2,1)S(1)} %get-tuple-element.9.col_ref) | copy-start | bytes 25165828
  95.1 2.2 %copy-start.2 = (bf16[16,144,1024]{2,1,0:T(8,128)(2,1)}, bf16[16,144,1024]{2,1,0:T(8,128)(2,1)S(1)}, u32[]{:S(2)}) copy-start(bf16[16,144,1024]{2,1,0:T(8,128)(2,1)S(1)} %get-tuple-element.8.row_ref) | copy-start | bytes 14155780
  97.3 3.4 %copy-start.1 = (bf16[16,1024,256]{2,1,0:T(8,128)(2,1)S(1)}, bf16[16,1024,256]{2,1,0:T(8,128)(2,1)}, u32[]{:S(2)}) copy-start(bf16[16,1024,256]{2,1,0:T(8,128)(2,1)} %copy-done) | copy-start | bytes 25165828
  100.7 2.3 %copy-start.3 = (bf16[16,144,1024]{2,1,0:T(8,128)(2,1)S(1)}, bf16[16,144,1024]{2,1,0:T(8,128)(2,1)}, u32[]{:S(2)}) copy-start(bf16[16,144,1024]{2,1,0:T(8,128)(2,1)} %copy-done.2) | copy-start | bytes 14155780
